TPU v7x, 128 devices: a whole 4x4x4 slice. The times are simulated.
128 devices in a mesh: frame: 16 (over y, x_hi, core), head: 8 (over x_lo, z).
Axes of the slice: x: 4 (x_hi: 2, x_lo: 2; x = x_hi * 2 + x_lo), y: 4, z: 4, core: 2. Of those that a mesh axis runs over, the one named last changes fastest.
Arguments:
- latents: bfloat16 [32, 1536, 1152], P('frame', 'head'), may hold values from -6 to 6
- modulation: float32 [6, 1152], replicated, may hold values from -3 to 3
- spatial_qkv: bfloat16 [1152, 3456], replicated, may hold values from -1 to 1
- spatial_out: bfloat16 [1152, 1152], replicated, may hold values from -0.1875 to 0.1875
- temporal_qkv: bfloat16 [1152, 3456], replicated, may hold values from -1 to 1
- temporal_out: bfloat16 [1152, 1152], replicated, may hold values from -0.1875 to 0.1875
Outputs:
- block_out: bfloat16 [32, 1536, 1152], P('frame', 'head')
All inputs are finite; a program needn't handle non-finite values.
Results may differ from a plain program's by a relative error of at most 0.015.
Values may be sent and summed in bfloat16 or wider, within the bound.
A program may use at most 192 MiB of HBM per device.

v0:
```python
import math

import jax
import jax.numpy as jnp
from jax import lax
from jax.sharding import PartitionSpec as P

HD = 72


def normalize(tokens, offset, stretch):
    values = tokens.astype(jnp.float32)
    average = jnp.mean(values, axis=-1, keepdims=True)
    centered = values - average
    variance = jnp.mean(centered * centered, axis=-1, keepdims=True)
    normed = centered * lax.rsqrt(variance + 1e-06)
    return (normed * (1.0 + offset * 0.0 + stretch) + offset).astype(jnp.bfloat16)


def rotate(tensor, frames):
    half = tensor.shape[-1] // 2
    inverse = 10000.0 ** (-jnp.arange(half, dtype=jnp.float32) / half)
    angles = jnp.arange(frames, dtype=jnp.float32)[:, None] * inverse[None, :]
    angle_cos = jnp.cos(angles)[:, None, None, :]
    angle_sin = jnp.sin(angles)[:, None, None, :]
    leading = tensor[..., :half].astype(jnp.float32)
    trailing = tensor[..., half:].astype(jnp.float32)
    turned = jnp.concatenate(
        [leading * angle_cos - trailing * angle_sin, leading * angle_sin + trailing * angle_cos], -1
    )
    return turned.astype(jnp.bfloat16)


def attend(queries, keys, values):
    scores = jnp.einsum(
        "qbhe,kbhe->bhqk", queries, keys, preferred_element_type=jnp.float32
    ) / math.sqrt(HD)
    weights_bf = jax.nn.softmax(scores, axis=-1).astype(jnp.bfloat16)
    mixed = jnp.einsum("bhqk,kbhe->qbhe", weights_bf, values, preferred_element_type=jnp.float32)
    return mixed.astype(jnp.bfloat16)


def temporal_heads(projected):
    frames, patches, columns = projected.shape
    heads_all = columns // (3 * HD)
    pieces = projected.reshape(frames, patches, 3, heads_all, HD)
    queries = rotate(pieces[:, :, 0], frames)
    keys_rot = rotate(pieces[:, :, 1], frames)
    outputs = attend(queries, keys_rot, pieces[:, :, 2])
    return outputs.reshape(frames, patches, heads_all * HD)


def local(latents, modulation, spatial_qkv, spatial_out, temporal_qkv, temporal_out):
    head_count = lax.axis_size("head")
    frame_count = lax.axis_size("frame")
    frames, patches, features = latents.shape
    columns = features // head_count
    portion = patches // frame_count
    normed = normalize(latents, modulation[0], modulation[1])
    projected = jnp.dot(
        normed.reshape(frames * patches, features), spatial_qkv, preferred_element_type=jnp.float32
    )
    projected = projected.astype(jnp.bfloat16).reshape(frames, patches, 3, head_count, columns)
    gathered = lax.all_to_all(projected, "head", split_axis=3, concat_axis=1, tiled=True)
    frame_items = gathered.shape[0]
    whole = gathered.shape[1]
    pieces = gathered.reshape(frame_items, whole, 3, columns // HD, HD).transpose(1, 0, 2, 3, 4)
    outputs = attend(pieces[:, :, 0], pieces[:, :, 1], pieces[:, :, 2])
    attended = outputs.transpose(1, 0, 2, 3).reshape(frame_items, whole, 1, columns)
    returned = lax.all_to_all(attended, "head", split_axis=1, concat_axis=2, tiled=True)
    projection = jnp.dot(
        returned.reshape(frames * patches, features),
        spatial_out,
        preferred_element_type=jnp.float32,
    )
    middle = (
        latents.astype(jnp.float32) + modulation[2] * projection.reshape(frames, patches, features)
    ).astype(jnp.bfloat16)
    normed_mid = normalize(middle, modulation[3], modulation[4])
    projected_mid = jnp.dot(
        normed_mid.reshape(frames * patches, features),
        temporal_qkv,
        preferred_element_type=jnp.float32,
    )
    projected_mid = projected_mid.astype(jnp.bfloat16).reshape(
        frames, frame_count, portion, 3 * features
    )
    outputs = temporal_heads(
        lax.all_to_all(projected_mid, "frame", split_axis=1, concat_axis=0, tiled=True)[:, 0]
    )
    returned_mid = lax.all_to_all(
        outputs[:, None], "frame", split_axis=0, concat_axis=1, tiled=True
    )
    projection_mid = jnp.dot(
        returned_mid.reshape(frames * patches, features),
        temporal_out,
        preferred_element_type=jnp.float32,
    )
    finished = middle.astype(jnp.float32) + modulation[5] * projection_mid.reshape(
        frames, patches, features
    )
    return finished.astype(jnp.bfloat16)


def solution(mesh):
    return jax.shard_map(
        local,
        mesh=mesh,
        in_specs=(P("frame", "head", None), P(), P(), P(), P(), P()),
        out_specs=P("frame", "head", None),
        check_vma=False,
    )
```

profile of v0, /device:TPU:1, one launch (start us, length us, event | category | flops | bytes accessed | tf_op | source)
XLA Modules:
  0.0 297.2 jit_solution(531716248859137823)
XLA Ops:
  0.0 0.0 copy-start
  0.0 1.8 slice_reduce_fusion.2
  1.8 1.4 convert_reduce_fusion
  3.1 1.5 fusion.28
  4.7 0.6 add_add_fusion
  5.3 1.6 fusion.31
  6.9 8.3 %convolution_convert_fusion.1 = bf16[384,3456]{1,0:T(8,128)(2,1)} fusion(bf16[384,1152]{1,0:T(8,128)(2,1)S(1)} %bitcast.84, bf16[1152,3456]{1,0:T(8,128)(2,1)} %param.8), kind=kOutput, calls=%fused_computation.9 | convolution fusion | flops 3058974720 | bytes 11501568 | tf_op jit(solution)/shard_map/dot_general | solution.py:60
  15.1 9.5 %reshape.132 = bf16[2,192,3,8,144]{4,3,2,1,0:T(8,128)(2,1)} reshape(bf16[384,3456]{1,0:T(8,128)(2,1)} %convolution_convert_fusion.1) | data formatting | bytes 5308416 | tf_op jit(solution)/shard_map/reshape | solution.py:63
  24.6 11.4 %copy.37 = bf16[2,192,3,8,144]{1,0,4,2,3:T(2,128)(2,1)} copy(bf16[2,192,3,8,144]{4,3,2,1,0:T(8,128)(2,1)} %reshape.132) | data formatting | bytes 5308416 | tf_op jit(solution)/shard_map/reshape | solution.py:63
  36.0 48.1 %all_to_all.60 = bf16[2,192,3,8,144]{1,0,4,2,3:T(2,128)(2,1)S(1)} all-to-all(bf16[2,192,3,8,144]{1,0,4,2,3:T(2,128)(2,1)} %copy.37), channel_id=1, replica_groups=mesh['frame'=16,'head'=8] {'head'}, dimensions={3} | all-to-all | bytes 5308416 | tf_op jit(solution)/shard_map/all_to_all | solution.py:64
  84.1 3.8 %copy.38 = bf16[2,8,192,3,1,144]{2,1,5,0,3,4:T(8,128)(2,1)} copy(bf16[2,8,192,3,1,144]{2,0,5,3,1,4:T(2,128)(2,1)S(1)} %bitcast.75) | data formatting | bytes 5308416 | tf_op jit(solution)/shard_map/all_to_all | solution.py:64
  87.9 6.4 %reshape.126 = bf16[2,1536,3,2,72]{1,4,3,0,2:T(8,128)(2,1)} reshape(bf16[2,8,192,3,1,144]{2,1,5,0,3,4:T(8,128)(2,1)} %copy.38) | data formatting | bytes 5308416 | tf_op jit(solution)/shard_map/reshape | solution.py:67
  94.4 20.4 %fusion.50 = (f32[2,2,1536]{2,1,0:T(2,128)}, f32[2,2,1536,1536]{2,3,1,0:T(8,128)}) fusion(bf16[1536,2,3,2,72]{0,4,3,1,2:T(8,128)(2,1)} %bitcast.82), kind=kOutput, calls=%fused_computation.91 | convolution fusion | flops 1387267584 | bytes 39542784 | tf_op jit(solution)/shard_map/sub | solution.py:38
  114.7 13.8 %fusion.25 = bf16[2,2,72,1536]{3,2,1,0:T(8,128)(2,1)S(1)} fusion(f32[2,2,1536,1536]{2,3,1,0:T(8,128)} %get-tuple-element.23, f32[2,2,1536]{2,1,0:T(2,128)} %get-tuple-element.22, bf16[1536,2,3,2,72]{0,4,3,1,2:T(8,128)(2,1)} %bitcast.83), kind=kOutput, calls=%fused_computation.42 | convolution fusion | flops 1378271232 | bytes 39542784 | tf_op jit(solution)/shard_map/bhqk,kbhe->qbhe/dot_general | solution.py:39
  128.6 2.9 copy.40
  131.4 0.0 copy-start.3
  131.4 22.6 %all_to_all.61 = bf16[2,1536,1,144]{3,0,2,1:T(2,128)(2,1)} all-to-all(bf16[2,1536,1,144]{3,0,2,1:T(2,128)(2,1)} %copy.40), channel_id=1, replica_groups=mesh['frame'=16,'head'=8] {'head'}, dimensions={1} | all-to-all | bytes 1769472 | tf_op jit(solution)/shard_map/all_to_all | solution.py:70
  154.0 5.0 %copy.61 = bf16[2,8,192,1,144]{2,4,1,0,3:T(8,128)(2,1)} copy(bf16[2,8,192,1,144]{4,0,2,1,3:T(2,128)(2,1)} %bitcast.79) | data formatting | bytes 1769472 | tf_op jit(solution)/shard_map/all_to_all | solution.py:70
  159.1 0.0 copy-done
  159.1 0.0 copy-done.3
  159.1 0.0 copy-start.4
  159.1 2.9 fusion.51
  162.0 0.0 copy-start.1
  162.1 0.3 multiply_reduce_fusion.2
  162.4 1.0 copy-done.1
  163.4 0.0 copy-done.4
  163.4 0.4 add_convert_fusion
  163.7 8.3 %convolution_convert_fusion = bf16[384,3456]{1,0:T(8,128)(2,1)} fusion(bf16[384,1152]{1,0:T(8,128)(2,1)S(1)} %bitcast.87, bf16[1152,3456]{1,0:T(8,128)(2,1)} %param.10), kind=kOutput, calls=%fused_computation.8 | convolution fusion | flops 3058974720 | bytes 11501568 | tf_op jit(solution)/shard_map/dot_general | solution.py:80
  172.0 5.2 %reshape.129 = bf16[2,16,12,3456]{3,2,1,0:T(8,128)(2,1)} reshape(bf16[384,3456]{1,0:T(8,128)(2,1)} %convolution_convert_fusion) | data formatting | bytes 5308416 | tf_op jit(solution)/shard_map/reshape | solution.py:85
  177.2 6.2 %copy.44 = bf16[2,16,12,3456]{3,0,2,1:T(2,128)(2,1)} copy(bf16[2,16,12,3456]{3,2,1,0:T(8,128)(2,1)} %reshape.129) | data formatting | bytes 5308416 | tf_op jit(solution)/shard_map/reshape | solution.py:85
  183.5 10.9 %all-to-all-start.2 = ((bf16[2,16,12,3456]{3,0,2,1:T(2,128)(2,1)}), bf16[2,16,12,3456]{3,0,2,1:T(2,128)(2,1)}, u32[]{:S(2)}, u32[]{:S(2)}) async-start(bf16[2,16,12,3456]{3,0,2,1:T(2,128)(2,1)} %copy.44), calls=%async_computation.2 | async-start | bytes 5308416 | tf_op jit(solution)/shard_map/all_to_all | solution.py:89
  194.3 0.1 fusion.45
  194.4 34.5 %all-to-all-done.2 = bf16[2,16,12,3456]{3,0,2,1:T(2,128)(2,1)} async-done(((bf16[2,16,12,3456]{3,0,2,1:T(2,128)(2,1)}), bf16[2,16,12,3456]{3,0,2,1:T(2,128)(2,1)}, u32[]{:S(2)}, u32[]{:S(2)}) %all-to-all-start.2) | async-done | bytes 2654240 | tf_op jit(solution)/shard_map/all_to_all | solution.py:89
  228.9 5.1 %copy.45 = bf16[16,2,1,12,3456]{4,1,0,3,2:T(2,128)(2,1)} copy(bf16[16,2,1,12,3456]{4,1,3,0,2:T(2,128)(2,1)} %bitcast.16) | data formatting | bytes 5308416 | tf_op jit(solution)/shard_map/all_to_all | solution.py:89
  234.0 13.2 %reshape_squeeze.3 = bf16[32,12,3,16,72]{4,3,2,0,1:T(8,128)(2,1)} reshape(bf16[16,2,1,12,3456]{4,1,0,3,2:T(2,128)(2,1)} %copy.45) | data formatting | bytes 5308416 | tf_op jit(solution)/shard_map/reshape;squeeze | solution.py:46
  247.3 3.5 %fusion.49 = (bf16[32,12,1,16,72]{4,3,2,0,1:T(8,128)(2,1)S(1)}, bf16[32,12,1,16,72]{4,3,2,0,1:T(8,128)(2,1)S(1)}, bf16[32,12,1,16,72]{4,3,2,0,1:T(8,128)(2,1)S(1)}) fusion(bf16[32,12,3,16,72]{4,3,2,0,1:T(8,128)(2,1)} %reshape_squeeze.3), kind=kLoop, calls=%fused_computation.90 | loop fusion | bytes 5308416 | tf_op jit(solution)/shard_map/slice | solution.py:49
  250.7 0.4 copy.77
  251.2 0.4 copy.78
  251.6 2.6 fusion.12
  254.2 1.7 fusion.32
  255.9 7.2 %fusion.52 = (f32[12,16,32]{2,1,0:T(8,128)S(1)}, f32[12,16,32,32]{2,3,1,0:T(8,128)S(1)}) fusion(f32[12,16,32,32]{2,3,1,0:T(8,128)S(1)} %fusion.32), kind=kOutput, calls=%fused_computation.93 | output fusion | flops 786463 | bytes 1597440 | tf_op jit(solution)/shard_map/sub | solution.py:38
  263.1 0.8 fusion.41
  264.0 1.8 copy.62
  265.7 4.2 %reshape.133 = bf16[32,1,12,1152]{3,2,1,0:T(8,128)(2,1)} reshape(bf16[32,12,16,72]{3,2,1,0:T(8,128)(2,1)} %copy.62) | data formatting | bytes 1769472 | tf_op jit(solution)/shard_map/broadcast_in_dim;reshape | solution.py:92
  269.9 0.0 copy-start.2
  269.9 0.0 copy-start.5
  269.9 0.0 copy-start.6
  269.9 23.6 %all_to_all.62 = bf16[32,1,12,1152]{3,2,1,0:T(8,128)(2,1)S(1)} all-to-all(bf16[32,1,12,1152]{3,2,1,0:T(8,128)(2,1)} %reshape.133), channel_id=1, replica_groups=mesh['frame'=16,'head'=8] {'frame'}, dimensions={0} | all-to-all | bytes 1769472 | tf_op jit(solution)/shard_map/all_to_all | solution.py:91
  293.5 0.7 copy.79
  294.2 0.6 copy.53
  294.9 0.0 copy-done.2
  294.9 0.0 copy-done.5
  294.9 0.0 copy-done.6
  294.9 2.4 fusion.17
  (5 shorter events, 0.0 us)
Async XLA Ops:
  0.0 159.1 %copy-start = (bf16[1152,1152]{1,0:T(8,128)(2,1)S(1)}, bf16[1152,1152]{1,0:T(8,128)(2,1)}, u32[]{:S(2)}) copy-start(bf16[1152,1152]{1,0:T(8,128)(2,1)} %param.9) | copy-start | bytes 7962628
  131.4 27.7 %copy-start.3 = (bf16[2,192,1152]{2,1,0:T(8,128)(2,1)S(1)}, bf16[2,192,1152]{2,1,0:T(8,128)(2,1)}, u32[]{:S(2)}) copy-start(bf16[2,192,1152]{2,1,0:T(8,128)(2,1)} %param.6) | copy-start | bytes 2654212
  159.1 4.3 %copy-start.4 = (f32[1152]{0:T(1024)S(1)}, f32[1152]{0:T(1024)}, u32[]{:S(2)}) copy-start(f32[1152]{0:T(1024)} %get-tuple-element.28) | copy-start | bytes 13828
  162.0 1.3 copy-start.1
  183.5 45.5 %all-to-all-start.2 = ((bf16[2,16,12,3456]{3,0,2,1:T(2,128)(2,1)}), bf16[2,16,12,3456]{3,0,2,1:T(2,128)(2,1)}, u32[]{:S(2)}, u32[]{:S(2)}) async-start(bf16[2,16,12,3456]{3,0,2,1:T(2,128)(2,1)} %copy.44), calls=%async_computation.2 | async-start | bytes 5308416 | tf_op jit(solution)/shard_map/all_to_all | solution.py:89
  269.9 24.9 %copy-start.2 = (f32[2,192,1152]{2,1,0:T(8,128)S(1)}, f32[2,192,1152]{2,1,0:T(8,128)}, u32[]{:S(2)}) copy-start(f32[2,192,1152]{2,1,0:T(8,128)} %copy-done.1) | copy-start | bytes 5308420
  269.9 25.0 %copy-start.5 = (f32[1152]{0:T(1024)S(1)}, f32[1152]{0:T(1024)}, u32[]{:S(2)}) copy-start(f32[1152]{0:T(1024)} %get-tuple-element.5) | copy-start | bytes 13828
  269.9 25.0 %copy-start.6 = (bf16[1152,1152]{1,0:T(8,128)(2,1)S(1)}, bf16[1152,1152]{1,0:T(8,128)(2,1)}, u32[]{:S(2)}) copy-start(bf16[1152,1152]{1,0:T(8,128)(2,1)} %param.11) | copy-start | bytes 7962628
where the time goes:
time: 299 us; the launch traced here: 297 us
  blocking collectives  94.4 us (32%)
  local copies, waits for them, and re-layouts  83.1 us (28%)
  matrix products  58.6 us (20%)
  waiting for transfers between devices  34.5 us (12%)
  other arithmetic  15.6 us (5%)
  starting transfers between devices  10.9 us (4%)
    all_to_all x1, blocking collectives, local(): lax.all_to_all(projected, 'head', split_axis=3, concat_axis=1, tiled=True)  48.1 us
    all_to_all x1, waiting for transfers between devices, local(): lax.all_to_all(projected_mid, 'frame', split_axis=1, concat_axis=0, tiled...  34.5 us
    all_to_all x1, blocking collectives, local(): lax.all_to_all(outputs[:, None], 'frame', split_axis=0, concat_axis=1, ti...  23.6 us
    all_to_all x1, blocking collectives, local(): lax.all_to_all(attended, 'head', split_axis=1, concat_axis=2, tiled=True)  22.6 us
    reshape x2, local copies, waits for them, and re-layouts, local(): projected.astype(jnp.bfloat16)  20.9 us
    sub x1, matrix products, attend(): weights_bf = jax.nn.softmax(scores, axis=-1).astype(jnp.bfloat16)  20.4 us
    dot_general x2, matrix products, attend(): jnp.einsum('bhqk,kbhe->qbhe', weights_bf, values, preferred_element_type=...  14.6 us
    another operation x1, local copies, waits for them, and re-layouts, temporal_heads(): pieces = projected.reshape(frames, patches, 3, heads_all, HD)  13.2 us
  transfers between devices with their start and end apart: 1, of which 1 were waited for; matrix products, arithmetic and copies ran while one was open for 0% of the time, Pallas kernels for 0%

commit v1 on v0

v1 whole, which is shorter than its diff:
```python
import math

import jax
import jax.numpy as jnp
import numpy as np
from jax import lax
from jax.experimental import pallas as pl
from jax.experimental.pallas import tpu as pltpu
from jax.sharding import PartitionSpec as P

MESH = pl.DeviceIdType.MESH
BF = jnp.bfloat16
F32 = jnp.float32
D, H, HD, F = 1152, 16, 72, 32
NH, NF = 8, 16
PAIR = 2 * HD
PATCH = 192
TOK = 2 * PATCH
KEYS = NH * PATCH
WIN = 5 * 128
SCALE = math.log2(math.e) / math.sqrt(HD)
NN = (((1,), (0,)), ((), ()))
NT = (((1,), (1,)), ((), ()))


def dot(a, b, dims=NN):
    return lax.dot_general(a, b, dims, preferred_element_type=F32)


def rope_table():
    inverse = 10000.0 ** (-np.arange(HD // 2) / (HD // 2))
    angles = np.arange(F)[:, None] * inverse[None, :]
    zeros = np.zeros_like(angles)
    cos = np.tile(np.concatenate([np.cos(angles)] * 2, 1), (1, H))
    low = np.tile(np.concatenate([-np.sin(angles), zeros], 1), (1, H))
    high = np.tile(np.concatenate([zeros, np.sin(angles)], 1), (1, H))
    rows = [t.reshape(NF, 2, D) for t in (cos, low, high, np.zeros((F, D)))]
    return np.concatenate(rows, 1).astype(np.float32)


def norm(x, offset, stretch):
    centered = x - jnp.mean(x, axis=-1, keepdims=True)
    variance = jnp.mean(centered * centered, axis=-1, keepdims=True)
    return centered * lax.rsqrt(variance + 1e-06) * (1.0 + stretch) + offset


def kernel(
    lat_h, mod, tab_h, wsq_h, wso_h, wtq_h, wto_h, out,
    lat, tab, wsq, wso, wtq, wto, load_sem,
    nrm, proj, recv, ks, vs, qs, sc, ob, ot, orecv, oa, mid, tin,
    ts, tsh, tr, trh, acc, acch, to, toh, ro, roh, bias,
    s_send, s_recv, r_send, r_recv, t_send, t_recv, th_send, th_recv,
    u_send, u_recv, uh_send, uh_recv,
):
    fi, hi = lax.axis_index("frame"), lax.axis_index("head")

    def at_head(k):
        return lax.rem(hi + k, NH)

    def at_frame(k):
        return lax.rem(fi + k, NF)

    def load(src, dst, i):
        return pltpu.make_async_copy(src, dst, load_sem.at[i])

    part_loads = [
        load(wsq_h.at[:, pl.ds(p * D, D)], wsq.at[:, pl.ds(p * D, D)], 2 + p) for p in range(3)
    ]
    loads = [
        load(lat_h, lat, 0), load(tab_h.at[fi], tab, 1), *part_loads,
        load(wso_h, wso, 5), load(wtq_h, wtq, 6), load(wto_h, wto, 7),
    ]
    for i in (0, 3, 4, 2, 1, 5, 6, 7):
        loads[i].start()

    barrier = pltpu.get_barrier_semaphore()

    def greet(k, _):
        pl.semaphore_signal(barrier, inc=1, device_id=(fi, at_head(k)), device_id_type=MESH)
        return 0

    def greet_frame(k, _):
        pl.semaphore_signal(barrier, inc=1, device_id=(at_frame(k), hi), device_id_type=MESH)
        return 0

    lax.fori_loop(1, NH, greet, 0)
    lax.fori_loop(1, NF, greet_frame, 0)

    def remote(src, dst, send, receive, device):
        return pltpu.make_async_remote_copy(
            src_ref=src, dst_ref=dst, send_sem=send, recv_sem=receive,
            device_id=device, device_id_type=MESH,
        )

    def await_bytes(ref, sem):
        pltpu.make_async_copy(ref, ref, sem).wait()

    loads[0].wait()
    for row, f, p, n in ((0, 0, 0, 128), (128, 1, 0, 128), (256, 0, 128, 64), (320, 1, 128, 64)):
        x = lat[f, p : p + n].astype(F32)
        nrm[row : row + n] = norm(x, mod[0:1], mod[1:2]).astype(BF)

    def piece(kind, ref, block):
        if kind < 2:
            return ref.at[kind, block]
        return ref.at[2, block, :, pl.ds(0, 256) if kind == 2 else pl.ds(256, 128)]

    def spatial_send(kinds):
        for kind in kinds:
            pltpu.make_async_copy(
                piece(kind, proj, hi), piece(kind, recv, hi), s_recv.at[kind, hi]
            ).start()

            def send(k, _):
                peer = at_head(k)
                remote(
                    piece(kind, proj, peer), piece(kind, recv, hi),
                    s_send.at[kind, peer], s_recv.at[kind, hi], (fi, peer),
                ).start()
                return 0

            lax.fori_loop(1, NH, send, 0)

    for slot, part in enumerate((1, 2, 0)):
        part_loads[part].wait()
        r = dot(nrm[...], wsq[:, part * D : (part + 1) * D])
        proj[slot] = r.astype(BF).T.reshape(NH, PAIR, TOK)
        if slot == 0:
            pl.semaphore_wait(barrier, NH + NF - 2)
        spatial_send(((0,), (1,), (2, 3))[slot])

    row = lax.broadcasted_iota(jnp.int32, (256, 256), 0) % 8
    col = lax.broadcasted_iota(jnp.int32, (256, 256), 1) % 8
    bias[...] = jnp.where(row == col, 0.0, -jnp.inf).astype(F32)

    vs[:, PAIR:, :] = jnp.ones((2, 16, KEYS), BF)
    lane = lax.broadcasted_iota(jnp.int32, (PAIR, 128), 1)

    def gather(kind, ref):
        def body(j, _):
            halves = []
            for b in range(2):
                src = 2 * j + b
                await_bytes(recv.at[kind, src], s_recv.at[kind, src])
                for f in range(2):
                    at = pl.multiple_of(src * 128, 128)
                    ref[f, 0:PAIR, pl.ds(at, 128)] = recv[kind, src, :, f * 128 : f * 128 + 128]
                halves.append(recv[kind, src, :, 256:384].astype(F32))
            a, b = halves
            at = pl.multiple_of(1024 + j * 128, 128)
            first = jnp.where(lane < 64, a, pltpu.roll(b, 64, 1))
            second = jnp.where(lane < 64, pltpu.roll(a, 64, 1), b)
            ref[0, 0:PAIR, pl.ds(at, 128)] = first.astype(BF)
            ref[1, 0:PAIR, pl.ds(at, 128)] = second.astype(BF)
            return 0

        lax.fori_loop(0, NH // 2, body, 0)

    gather(0, ks)
    gather(1, vs)

    def pair_source(i, b):
        return 2 * lax.rem(hi // 2 + i, 4) + b

    def quad_source(i, b):
        return 4 * lax.rem(hi // 4 + i - 4, 2) + b

    def take_pair(i):
        for b in range(2):
            src = pair_source(i, b)
            await_bytes(piece(2, recv, src), s_recv.at[2, src])
            for f in range(2):
                qs[i, f, b * 128 : b * 128 + 128] = recv[2, src, :, f * 128 : f * 128 + 128].T

    def take_quad(i):
        for b in range(4):
            src = quad_source(i, b)
            await_bytes(piece(3, recv, src), s_recv.at[3, src])
            q = recv[2, src, :, 256:384].T
            for f in range(2):
                qs[i, f, b * 64 : b * 64 + 64] = q[f * 64 : f * 64 + 64]

    column = lax.broadcasted_iota(jnp.int32, (256, PAIR), 1)

    def scores(i, f, h):
        q = qs[i, f]
        own = (column < HD) if h == 0 else (column >= HD)
        return dot(jnp.where(own, q, jnp.zeros_like(q)), ks[f])

    def mixed(s, f):
        p = jnp.exp2((s - jnp.max(s, axis=1, keepdims=True)) * SCALE).astype(BF)
        o = dot(p, vs[f], NT)
        return o[:, 0:PAIR] * (1.0 / o[:, PAIR : PAIR + 1])

    def give(kind, src):
        lanes = pl.ds(0, 256) if kind == 0 else pl.ds(256, 128)
        here, there = ot.at[src, :, lanes], orecv.at[hi, :, lanes]

        @pl.when(src == hi)
        def _():
            pltpu.make_async_copy(here, there, r_recv.at[kind, hi]).start()

        @pl.when(src != hi)
        def _():
            remote(here, there, r_send.at[kind, src], r_recv.at[kind, hi], (fi, src)).start()

    take_pair(0)
    sc[0] = scores(0, 0, 0)

    def attend(i, _):
        first = None
        for u in range(4):
            f, h = u // 2, u % 2
            if u == 3:

                @pl.when(i < 3)
                def _():
                    take_pair(i + 1)

                @pl.when((i >= 3) & (i < 5))
                def _():
                    take_quad(i + 1)

            later = jnp.minimum(i + 1, 5) if u == 3 else i
            s = sc[u % 2]
            sc[(u + 1) % 2] = scores(later, (u + 1) % 4 // 2, (u + 1) % 2)
            o = mixed(s, f)
            if h == 0:
                first = o
            else:
                ob[f] = jnp.where(column < HD, first, o).astype(BF)

        @pl.when(i < 4)
        def _():
            for f in range(2):
                o = ob[f].T
                for b in range(2):
                    ot[pair_source(i, b), :, f * 128 : f * 128 + 128] = o[:, b * 128 : b * 128 + 128]
            for b in range(2):
                give(0, pair_source(i, b))

        @pl.when(i >= 4)
        def _():
            for b in range(4):
                rows = pl.ds(b * 64, 64)
                o = jnp.concatenate([ob[0, rows], ob[1, rows]], 0)
                ot[quad_source(i, b), :, 256:384] = o.T
            for b in range(4):
                give(1, quad_source(i, b))

        return 0

    lax.fori_loop(0, 6, attend, 0)

    for i in (1, 5, 6):
        loads[i].wait()

    def finish_spatial(kind):
        def arrive(src, _):
            lanes = pl.ds(0, 256) if kind == 0 else pl.ds(256, 128)
            await_bytes(orecv.at[src, :, lanes], r_recv.at[kind, src])
            return 0

        lax.fori_loop(0, NH, arrive, 0)
        start, count = ((0, 256), (256, 128))[kind]
        for t in range(count // 128):
            at = start + t * 128
            oa[at : at + 128] = orecv[:, :, at : at + 128].reshape(D, 128).T
        r = dot(oa[start : start + count], wso[...])
        half = count // 2
        first = 128 * kind
        fresh = []
        for f in range(2):
            x = lat[f, first : first + half].astype(F32)
            m = (x + mod[2:3] * r[f * half : (f + 1) * half]).astype(BF)
            mid[f, first : first + half] = m
            fresh.append(norm(m.astype(F32), mod[3:4], mod[4:5]))
        for g in range(half // 8):
            both = jnp.concatenate([x[g * 8 : g * 8 + 8] for x in fresh], 0)
            tin[start + g * 16 : start + g * 16 + 16] = both.astype(BF)

    def table(i):
        rows = [jnp.broadcast_to(tab[2 * i + f : 2 * i + f + 1], (8, D)) for f in range(2)]
        return jnp.concatenate(rows, 0)[None]

    def temporal_part(start, count, part):
        r = dot(tin[start : start + count], wtq[:, part * D : (part + 1) * D])
        groups = count // 16
        r = r.astype(BF)
        if part == 2:
            return r.reshape(groups, 16, D)
        r = r.astype(F32)
        low = pltpu.roll(r, D - HD // 2, 1).reshape(groups, 16, D)
        high = pltpu.roll(r, HD // 2, 1).reshape(groups, 16, D)
        r = r.reshape(groups, 16, D)
        return (r * table(0) + low * table(1) + high * table(2)).astype(BF)

    def main_part(part, ref, group):
        return ref.at[group, :, pl.ds(part * D, D)]

    finish_spatial(0)
    for part in range(3):
        ts[:, :, part * D : (part + 1) * D] = temporal_part(0, 256, part)
        pltpu.make_async_copy(
            main_part(part, ts, fi), main_part(part, tr, fi), t_recv.at[part, fi]
        ).start()

        def send_main(k, _):
            peer = at_frame(k)
            remote(
                main_part(part, ts, peer), main_part(part, tr, fi),
                t_send.at[part, peer], t_recv.at[part, fi], (peer, hi),
            ).start()
            return 0

        lax.fori_loop(1, NF, send_main, 0)

    finish_spatial(1)
    for part in range(3):
        r = temporal_part(256, 128, part)
        tsh[:, 0, :, part * WIN : (part + 1) * WIN] = r[:, :, 0:WIN]
        tsh[:, 1, :, part * WIN : (part + 1) * WIN] = r[:, :, D - WIN : D]
    pltpu.make_async_copy(tsh.at[fi // 2, lax.rem(fi, 2)], trh.at[fi], th_recv.at[fi]).start()

    def send_half(k, _):
        peer = at_frame(k)
        remote(
            tsh.at[peer // 2, lax.rem(peer, 2)], trh.at[fi],
            th_send.at[peer], th_recv.at[fi], (peer, hi),
        ).start()
        return 0

    lax.fori_loop(1, NF, send_half, 0)

    window = lax.broadcasted_iota(jnp.int32, (256, 256), 1)

    def temporal_head(source, width, offset, total):
        tile = jnp.minimum(offset // 128, width // 128 - 2)
        begin = offset - tile * 128
        own = (window >= begin) & (window < begin + HD)

        def part(i):
            at = pl.multiple_of(i * width + tile * 128, 128)
            return source[:, :, pl.ds(at, 256)].reshape(256, 256)

        q = part(0)
        s = dot(jnp.where(own, q, jnp.zeros_like(q)), part(1), NT) + bias[...]
        e = jnp.exp2((s - jnp.max(s, axis=1, keepdims=True)) * SCALE)
        o = dot(e.astype(BF), part(2)) * (1.0 / jnp.sum(e, axis=1, keepdims=True))
        lanes = pl.ds(pl.multiple_of(tile * 128, 128), 256)
        total[:, lanes] = jnp.where(own, o, total[:, lanes])

    acc[...] = jnp.zeros_like(acc)
    acch[...] = jnp.zeros_like(acch)

    def arrive_main(k, _):
        src = at_frame(k)
        for part in range(3):
            await_bytes(main_part(part, tr, src), t_recv.at[part, src])
        return 0

    lax.fori_loop(0, NF, arrive_main, 0)

    def main_heads(j, _):
        for b in range(4):
            temporal_head(tr, D, (4 * j + b) * HD, acc)
        return 0

    lax.fori_loop(0, H // 4, main_heads, 0)
    to[...] = acc[...].astype(BF).reshape(NF, 16, D)
    pltpu.make_async_copy(to.at[fi], ro.at[fi], u_recv.at[fi]).start()

    def return_main(k, _):
        peer = at_frame(k)
        remote(to.at[peer], ro.at[fi], u_send.at[peer], u_recv.at[fi], (peer, hi)).start()
        return 0

    lax.fori_loop(1, NF, return_main, 0)

    def arrive_half(k, _):
        src = at_frame(k)
        await_bytes(trh.at[src], th_recv.at[src])
        return 0

    lax.fori_loop(0, NF, arrive_half, 0)

    def half_heads(j, _):
        for b in range(4):
            temporal_head(trh, WIN, (4 * j + b) * HD + 64 * lax.rem(fi, 2), acch)
        return 0

    lax.fori_loop(0, H // 8, half_heads, 0)
    toh[...] = acch[...].astype(BF).reshape(NF, 16, WIN)

    def half_place(src):
        return roh.at[lax.rem(src, 2), src // 2]

    pltpu.make_async_copy(toh.at[fi], half_place(fi), uh_recv.at[fi]).start()

    def return_half(k, _):
        peer = at_frame(k)
        remote(toh.at[peer], half_place(fi), uh_send.at[peer], uh_recv.at[fi], (peer, hi)).start()
        return 0

    lax.fori_loop(1, NF, return_half, 0)

    loads[7].wait()

    def finish(r, first, half):
        for f in range(2):
            for j in range(half // 16):
                at = 32 * j + 8 * f
                rows = jnp.concatenate([r[at : at + 8], r[at + 16 : at + 24]], 0)
                here = slice(first + 16 * j, first + 16 * j + 16)
                out[f, here] = (mid[f, here].astype(F32) + mod[5:6] * rows).astype(BF)

    def back_main(k, _):
        src = at_frame(k)
        await_bytes(ro.at[src], u_recv.at[src])
        return 0

    lax.fori_loop(0, NF, back_main, 0)
    finish(dot(ro[...].reshape(256, D), wto[...]), 0, 128)

    def back_half(k, _):
        src = at_frame(k)
        await_bytes(half_place(src), uh_recv.at[src])
        return 0

    lax.fori_loop(0, NF, back_half, 0)
    r = dot(roh[0].reshape(128, WIN), wto[0:WIN]) + dot(roh[1].reshape(128, WIN), wto[D - WIN : D])
    finish(r, 128, 64)

    def sent_head(k, _):
        peer = at_head(k)
        for kind in range(4):
            await_bytes(piece(kind, proj, peer), s_send.at[kind, peer])
        for kind, lanes in ((0, pl.ds(0, 256)), (1, pl.ds(256, 128))):
            await_bytes(ot.at[peer, :, lanes], r_send.at[kind, peer])
        return 0

    lax.fori_loop(1, NH, sent_head, 0)

    def sent_frame(k, _):
        peer = at_frame(k)
        for part in range(3):
            await_bytes(main_part(part, ts, peer), t_send.at[part, peer])
        await_bytes(trh.at[peer], th_send.at[peer])
        await_bytes(to.at[peer], u_send.at[peer])
        await_bytes(toh.at[peer], uh_send.at[peer])
        return 0

    lax.fori_loop(1, NF, sent_frame, 0)


def local(latents, modulation, spatial_qkv, spatial_out, temporal_qkv, temporal_out):
    anywhere = pl.BlockSpec(memory_space=pl.ANY)
    vmem = pl.BlockSpec(memory_space=pltpu.VMEM)
    dma = pltpu.SemaphoreType.DMA
    return pl.pallas_call(
        kernel,
        out_shape=jax.ShapeDtypeStruct((2, PATCH, D), BF),
        in_specs=[anywhere, vmem] + [anywhere] * 5,
        out_specs=vmem,
        scratch_shapes=[
            pltpu.VMEM((2, PATCH, D), BF),
            pltpu.VMEM((8, D), F32),
            pltpu.VMEM((D, 3 * D), BF),
            pltpu.VMEM((D, D), BF),
            pltpu.VMEM((D, 3 * D), BF),
            pltpu.VMEM((D, D), BF),
            dma((8,)),
            pltpu.VMEM((TOK, D), BF),
            pltpu.VMEM((3, NH, PAIR, TOK), BF),
            pltpu.VMEM((3, NH, PAIR, TOK), BF),
            pltpu.VMEM((2, PAIR, KEYS), BF),
            pltpu.VMEM((2, PAIR + 16, KEYS), BF),
            pltpu.VMEM((6, 2, 256, PAIR), BF),
            pltpu.VMEM((2, 256, KEYS), F32),
            pltpu.VMEM((2, 256, PAIR), BF),
            pltpu.VMEM((NH, PAIR, TOK), BF),
            pltpu.VMEM((NH, PAIR, TOK), BF),
            pltpu.VMEM((TOK, D), BF),
            pltpu.VMEM((2, PATCH, D), BF),
            pltpu.VMEM((TOK, D), BF),
            pltpu.VMEM((NF, 16, 3 * D), BF),
            pltpu.VMEM((8, 2, 16, 3 * WIN), BF),
            pltpu.VMEM((NF, 16, 3 * D), BF),
            pltpu.VMEM((NF, 16, 3 * WIN), BF),
            pltpu.VMEM((256, D), F32),
            pltpu.VMEM((256, WIN), F32),
            pltpu.VMEM((NF, 16, D), BF),
            pltpu.VMEM((NF, 16, WIN), BF),
            pltpu.VMEM((NF, 16, D), BF),
            pltpu.VMEM((2, 8, 16, WIN), BF),
            pltpu.VMEM((256, 256), F32),
            dma((4, NH)), dma((4, NH)), dma((2, NH)), dma((2, NH)),
            dma((3, NF)), dma((3, NF)), dma((NF,)), dma((NF,)),
            dma((NF,)), dma((NF,)), dma((NF,)), dma((NF,)),
        ],
        compiler_params=pltpu.CompilerParams(
            collective_id=0, has_side_effects=True, vmem_limit_bytes=62 * 2**20
        ),
    )(
        latents, modulation, jnp.asarray(rope_table()),
        spatial_qkv, spatial_out, temporal_qkv, temporal_out,
    )


def solution(mesh):
    return jax.shard_map(
        local,
        mesh=mesh,
        in_specs=(P("frame", "head", None), P(), P(), P(), P(), P()),
        out_specs=P("frame", "head", None),
        check_vma=False,
    )
```

time: 299 us -> 107 us (0.36)
  Pallas kernels: 0 us -> 105 us
  blocking collectives: 94.4 us -> 0 us
  local copies, waits for them, and re-layouts: 83.1 us -> 2.15 us
  matrix products: 58.6 us -> 0 us
  waiting for transfers between devices: 34.5 us -> 0 us
  other arithmetic: 15.6 us -> 0 us
  starting transfers between devices: 10.9 us -> 0 us
    pallas_call x0 -> x1, Pallas kernels: none -> 105 us  [local(): pl.pallas_call(kernel, out_shape=jax.ShapeDtypeStruct((2, PATCH, D), BF),...]
    all_to_all x3 -> x0, blocking collectives: 94.4 us -> none  [the longest x1 48.1 us: local(): lax.all_to_all(projected, 'head', split_axis=3, concat_axis=1, tiled=True)]
    reshape x6 -> x0, local copies, waits for them, and re-layouts: 41.6 us -> none  [the longest x2 20.9 us: local(): projected.astype(jnp.bfloat16)]
    dot_general x7 -> x0, matrix products: 38.2 us -> none  [the longest x2 14.6 us: attend(): jnp.einsum('bhqk,kbhe->qbhe', weights_bf, values, preferred_element_type=...]
    all_to_all x1 -> x0, waiting for transfers between devices: 34.5 us -> none  [local(): lax.all_to_all(projected_mid, 'frame', split_axis=1, concat_axis=0, tiled...]
    sub x1 -> x0, matrix products: 20.4 us -> none  [attend(): weights_bf = jax.nn.softmax(scores, axis=-1).astype(jnp.bfloat16)]
    another operation x3 -> x0, local copies, waits for them, and re-layouts: 19.2 us -> none  [the longest x1 13.2 us: temporal_heads(): pieces = projected.reshape(frames, patches, 3, heads_all, HD)]
    all_to_all x5 -> x0, local copies, waits for them, and re-layouts: 15.3 us -> none  [the longest x1 5.11 us: local(): lax.all_to_all(projected_mid, 'frame', split_axis=1, concat_axis=0, tiled...]
  transfers between devices with their start and end apart: 1 -> 0, of which waited for: 1 -> 0; matrix products, arithmetic and copies ran while one was open for 0% -> 0% of each run, Pallas kernels for 0% -> 0%
where the time goes in v1:
time: 107 us
  Pallas kernels  105 us (98%)
  local copies, waits for them, and re-layouts  2.15 us (2%)
    pallas_call x1, Pallas kernels, local(): pl.pallas_call(kernel, out_shape=jax.ShapeDtypeStruct((2, PATCH, D), BF),...  105 us
    unnamed x1, local copies, waits for them, and re-layouts  2.15 us

profile of v1, /device:TPU:1, one launch (start us, length us, event | category | flops | bytes accessed | tf_op | source)
XLA Modules:
  0.0 106.9 jit_solution(3120506852596199010)
XLA Ops:
  0.0 104.7 %shard_map.73 = bf16[2,192,1152]{2,1,0:T(8,128)(2,1)} custom-call(bf16[2,192,1152]{2,1,0:T(8,128)(2,1)} %lat_h.1, f32[6,1152]{1,0:T(8,128)} %mod.1, f32[16,8,1152]{2,1,0:T(8,128)} %constant.2.clone.tab_h, bf16[1152,3456]{1,0:T(8,128)(2,1)} %wsq_h.1, bf16[1152,1152]{1,0:T(8,128)(2,1)} %wso_h.1, bf16[1152,3456]{1,0:T(8,128)(2,1)} %wtq_h.1, ...), custom_call_target="tpu_custom_call" | custom-call | tf_op jit(solution)/shard_map/pallas_call | solution.py:460
  104.7 2.1 %copy.9 = bf16[2,192,1152]{2,1,0:T(8,128)(2,1)} copy(bf16[2,192,1152]{2,1,0:T(8,128)(2,1)} %shard_map.73) | data formatting | bytes 1769472

commit v2 on v0

v2 whole, which is shorter than its diff:
```python
import math

import jax
import jax.numpy as jnp
import numpy as np
from jax import lax
from jax.experimental import pallas as pl
from jax.experimental.pallas import tpu as pltpu
from jax.sharding import PartitionSpec as P

MESH = pl.DeviceIdType.MESH
BF = jnp.bfloat16
F32 = jnp.float32
D, H, HD, F = 1152, 16, 72, 32
NH, NF = 8, 16
PAIR = 2 * HD
PATCH = 192
TOK = 2 * PATCH
KEYS = NH * PATCH
WIN = 5 * 128
SCALE = math.log2(math.e) / math.sqrt(HD)
NN = (((1,), (0,)), ((), ()))
NT = (((1,), (1,)), ((), ()))


def dot(a, b, dims=NN):
    return lax.dot_general(a, b, dims, preferred_element_type=F32)


def rope_table():
    inverse = 10000.0 ** (-np.arange(HD // 2) / (HD // 2))
    angles = np.arange(F)[:, None] * inverse[None, :]
    zeros = np.zeros_like(angles)
    cos = np.tile(np.concatenate([np.cos(angles)] * 2, 1), (1, H))
    low = np.tile(np.concatenate([-np.sin(angles), zeros], 1), (1, H))
    high = np.tile(np.concatenate([zeros, np.sin(angles)], 1), (1, H))
    rows = [np.concatenate([np.repeat(t, 8, 0), np.repeat(t, 4, 0)], 0) for t in (cos, low, high)]
    return np.stack(rows).astype(np.float32)


def norm(x, offset, stretch):
    centered = x - jnp.mean(x, axis=-1, keepdims=True)
    variance = jnp.mean(centered * centered, axis=-1, keepdims=True)
    return centered * lax.rsqrt(variance + 1e-06) * (1.0 + stretch) + offset


def kernel(
    lat_h, mod, tab_h, wsq_h, wso_h, wtq_h, wto_h, out,
    lat, tab, wsq, wso, wtq, wto, load_sem,
    nrm, proj, recv, ks, vs, qs, sc, ob, ot, orecv, oa,
    ts, tsh, tr, trh, mid, tin, tp, acc, to, toh, ro, roh, bias,
    s_send, s_recv, r_send, r_recv, t_send, t_recv, th_send, th_recv,
    u_send, u_recv, uh_send, uh_recv,
):
    fi, hi = lax.axis_index("frame"), lax.axis_index("head")

    def at_head(k):
        return lax.rem(hi + k, NH)

    def at_frame(k):
        return lax.rem(fi + k, NF)

    def load(src, dst, i):
        return pltpu.make_async_copy(src, dst, load_sem.at[i])

    part_loads = [
        load(wsq_h.at[:, pl.ds(p * D, D)], wsq.at[:, pl.ds(p * D, D)], 2 + p) for p in range(3)
    ]
    loads = [
        load(lat_h, lat, 0), load(tab_h, tab, 1), *part_loads,
        load(wso_h, wso, 5), load(wtq_h, wtq, 6), load(wto_h, wto, 7),
    ]
    for i in (0, 3, 4, 2):
        loads[i].start()

    barrier = pltpu.get_barrier_semaphore()

    def greet(k, _):
        pl.semaphore_signal(barrier, inc=1, device_id=(fi, at_head(k)), device_id_type=MESH)
        return 0

    def greet_frame(k, _):
        pl.semaphore_signal(barrier, inc=1, device_id=(at_frame(k), hi), device_id_type=MESH)
        return 0

    lax.fori_loop(1, NH, greet, 0)
    lax.fori_loop(1, NF, greet_frame, 0)

    def remote(src, dst, send, receive, device):
        return pltpu.make_async_remote_copy(
            src_ref=src, dst_ref=dst, send_sem=send, recv_sem=receive,
            device_id=device, device_id_type=MESH,
        )

    def await_bytes(ref, sem):
        pltpu.make_async_copy(ref, ref, sem).wait()

    loads[0].wait()
    for row, f, p, n in ((0, 0, 0, 192), (192, 1, 128, 64), (256, 1, 0, 128)):
        x = lat[f, p : p + n].astype(F32)
        nrm[row : row + n] = norm(x, mod[0:1], mod[1:2]).astype(BF)

    def piece(phase, ref, part, block):
        rows = (pl.ds(0, 80), pl.ds(80, 64))[phase % 2]
        lanes = (pl.ds(0, 256), pl.ds(256, 128))[phase // 2]
        return ref.at[part, block, rows, lanes]

    def spatial_send(phase, part):
        pltpu.make_async_copy(
            piece(phase, proj, part, hi), piece(phase, recv, part, hi), s_recv.at[phase, part, hi]
        ).start()

        def send(k, _):
            peer = at_head(k)
            remote(
                piece(phase, proj, part, peer), piece(phase, recv, part, hi),
                s_send.at[phase, part, peer], s_recv.at[phase, part, hi], (fi, peer),
            ).start()
            return 0

        lax.fori_loop(1, NH, send, 0)

    for slot, part in enumerate((1, 2, 0)):
        part_loads[part].wait()
        r = dot(nrm[...], wsq[:, part * D : (part + 1) * D])
        proj[slot] = r.astype(BF).T.reshape(NH, PAIR, TOK)
        if slot == 0:
            pl.semaphore_wait(barrier, NH + NF - 2)
        spatial_send(0, slot)
    for phase in range(1, 4):
        for slot in range(3):
            spatial_send(phase, slot)
    for i in (5, 6, 1, 7):
        loads[i].start()

    row = lax.broadcasted_iota(jnp.int32, (256, 256), 0)
    col = lax.broadcasted_iota(jnp.int32, (256, 256), 1)
    bias[0] = jnp.where(row % 8 == col % 8, 0.0, -jnp.inf).astype(F32)
    bias[1] = jnp.where(row % 4 == col % 4, 0.0, -jnp.inf).astype(F32)

    for rows in (slice(0, 16), slice(16 + PAIR, 32 + PAIR)):
        vs[:, rows, :] = jnp.ones((2, 16, KEYS), BF)

    def halves(a, b):
        a, b = a.astype(F32), b.astype(F32)
        lane = lax.broadcasted_iota(jnp.int32, a.shape, 1)
        first = jnp.where(lane < 64, a, pltpu.roll(b, 64, 1))
        second = jnp.where(lane < 64, pltpu.roll(a, 64, 1), b)
        return first.astype(BF), second.astype(BF)

    def prepare(f, h):
        phase = 2 * f + h
        lo, n = ((0, 80), (80, 64))[h]
        own = lax.broadcasted_iota(jnp.int32, (128, 80), 1)
        own = (own < HD) if h == 0 else (own >= 80 - HD)

        def body(j, _):
            sources = (2 * j, 2 * j + 1)
            for src in sources:
                for part in range(3):
                    await_bytes(piece(phase, recv, part, src), s_recv.at[phase, part, src])
            for part, ref, up in ((0, ks, 0), (1, vs, 16)):
                for src in sources:
                    at = pl.multiple_of(src * 128, 128)
                    lanes = slice(0, 128) if f == 0 else slice(256, 384)
                    ref[f, lo + up : lo + up + n, pl.ds(at, 128)] = recv[part, src, lo : lo + n, lanes]
                if f == 0:
                    at = pl.multiple_of(1024 + j * 128, 128)
                    tiles = halves(*(recv[part, src, lo : lo + n, 128:256] for src in sources))
                    for g in range(2):
                        ref[g, lo + up : lo + up + n, pl.ds(at, 128)] = tiles[g]
            for i, src in enumerate(sources):
                rows = slice(64 * h, 64 * h + 80)
                lanes = slice(0, 128) if f == 0 else slice(256, 384)
                q = recv[2, src, rows, lanes].T
                qs[j, i * 128 : i * 128 + 128] = jnp.where(own, q, jnp.zeros_like(q))
                q = recv[2, src, rows, 128:256].T[f * 64 : f * 64 + 64]
                q = jnp.where(own[0:64], q, jnp.zeros_like(q))
                qs[4 + j // 2, pl.ds(pl.multiple_of(j % 2 * 128 + i * 64, 64), 64)] = q
            return 0

        lax.fori_loop(0, NH // 2, body, 0)

    def scores(b, f, h):
        return dot(qs[b], ks[f, 64 * h : 64 * h + 80])

    def mixed(s, f, h):
        p = jnp.exp2((s - jnp.max(s, axis=1, keepdims=True)) * SCALE).astype(BF)
        o = dot(p, vs[f, 80 * h : 80 * h + 96], NT)
        one = 80 * h
        return (o * (1.0 / o[:, one : one + 1])).astype(BF)

    def back_piece(kind, ref, block):
        rows = (pl.ds(0, 64), pl.ds(64, 80))[kind % 2]
        return ref.at[block, rows, pl.ds(kind // 2 * 128, 128)]

    def give(kind, src):
        here, there = back_piece(kind, ot, src), back_piece(kind, orecv, hi)

        @pl.when(src == hi)
        def _():
            pltpu.make_async_copy(here, there, r_recv.at[kind, hi]).start()

        @pl.when(src != hi)
        def _():
            remote(here, there, r_send.at[kind, src], r_recv.at[kind, hi], (fi, src)).start()

    def put(src, h, lanes, o):
        if h == 0:
            ot[src, 0:80, lanes] = o[16:96]
        else:
            row = lax.broadcasted_iota(jnp.int32, (16, o.shape[1]), 0)
            ot[src, 64:80, lanes] = jnp.where(row < 8, ot[src, 64:80, lanes], o[0:16])
            ot[src, 80:PAIR, lanes] = o[16:80]

    def attend(f, h):
        prepare(f, h)
        sc[0] = scores(0, f, h)

        def body(j, _):
            for u in range(2):
                s = sc[u]
                sc[1 - u] = scores(jnp.minimum(2 * j + u + 1, 5), f, h)
                ob[u] = mixed(s, f, h)

            @pl.when(j < 2)
            def _():
                for u in range(2):
                    o = ob[u].T
                    for i in range(2):
                        src = 2 * (2 * j + u) + i
                        lanes = slice(0, 128) if f == 0 else slice(256, 384)
                        put(src, h, lanes, o[:, i * 128 : i * 128 + 128])
                        give(4 * f + h, src)

            @pl.when(j == 2)
            def _():
                for u in range(2):
                    for i in range(4):
                        src = 4 * u + i
                        o = ob[u, i * 64 : i * 64 + 64].T
                        put(src, h, slice(128 + 64 * f, 192 + 64 * f), o)
                        if f == 1:
                            give(2 + h, src)

            return 0

        lax.fori_loop(0, 3, body, 0)

    for f in range(2):
        for h in range(2):
            attend(f, h)

    for i in (1, 5):
        loads[i].wait()
    sub = lax.broadcasted_iota(jnp.int32, (8, D), 0)

    def swap(a, b):
        first = jnp.where(sub < 4, a, pltpu.roll(b, 4, 0))
        second = jnp.where(sub < 4, pltpu.roll(a, 4, 0), b)
        return first, second

    def pack(x):
        return jnp.concatenate([x[:, 0:WIN], x[:, D - WIN : D]], 0).astype(BF)

    def unpack(x):
        x = x.astype(F32)
        return jnp.concatenate([x[0:8], x[8:16, 2 * WIN - D : WIN]], 1)

    def finish_spatial(kind):
        kinds = ((0, 1, 4, 5), (2, 3))[kind]

        def arrive(src, _):
            for one in kinds:
                await_bytes(back_piece(one, orecv, src), r_recv.at[one, src])
            return 0

        lax.fori_loop(0, NH, arrive, 0)
        start, count = ((0, 256), (256, 128))[kind]
        for t, at in enumerate(((0, 256), (128,))[kind]):
            row = start + t * 128
            oa[row : row + 128] = orecv[:, :, at : at + 128].reshape(D, 128).T
        r = dot(oa[start : start + count], wso[...])
        half = count // 2
        first = 128 * kind
        fresh = []
        for f in range(2):
            x = lat[f, first : first + half].astype(F32)
            fresh.append(x + mod[2:3] * r[f * half : (f + 1) * half])
        for g in range(half // 8):
            a, b = (x[g * 8 : g * 8 + 8] for x in fresh)
            if kind == 0:
                ts[g] = jnp.concatenate([a, b], 0).astype(BF)
            else:
                a, b = swap(a, b)
                tsh[2 * g], tsh[2 * g + 1] = pack(a), pack(b)

    def exchange(source, target, send, receive):
        pltpu.make_async_copy(source.at[fi], target.at[fi], receive.at[fi]).start()

        def one(k, _):
            peer = at_frame(k)
            remote(
                source.at[peer], target.at[fi], send.at[peer], receive.at[fi], (peer, hi)
            ).start()
            return 0

        lax.fori_loop(1, NF, one, 0)

    def arrived(target, receive):
        def one(k, _):
            src = at_frame(k)
            await_bytes(target.at[src], receive.at[src])
            return 0

        lax.fori_loop(0, NF, one, 0)

    finish_spatial(0)
    exchange(ts, tr, t_send, t_recv)
    finish_spatial(1)
    exchange(tsh, trh, th_send, th_recv)

    def temporal_project(start, count):
        rows = slice(start, start + count)
        tin[rows] = norm(mid[rows], mod[3:4], mod[4:5]).astype(BF)
        for part in range(3):
            r = dot(tin[rows], wtq[:, part * D : (part + 1) * D]).astype(BF)
            if part < 2:
                r = r.astype(F32)
                low = pltpu.roll(r, D - HD // 2, 1)
                high = pltpu.roll(r, HD // 2, 1)
                r = (r * tab[0, rows] + low * tab[1, rows] + high * tab[2, rows]).astype(BF)
            tp[rows, part * D : (part + 1) * D] = r

    def temporal_head(start, count, offset):
        rows = slice(start, start + count)
        tile = jnp.minimum(offset // 128, 7)
        begin = offset - tile * 128
        lane = lax.broadcasted_iota(jnp.int32, (count, 256), 1)
        own = (lane >= begin) & (lane < begin + HD)

        def part(i):
            return tp[rows, pl.ds(pl.multiple_of(i * D + tile * 128, 128), 256)]

        q = part(0)
        s = dot(jnp.where(own, q, jnp.zeros_like(q)), part(1), NT)
        s = s + bias[0 if count == 256 else 1, 0:count, 0:count]
        e = jnp.exp2((s - jnp.max(s, axis=1, keepdims=True)) * SCALE)
        o = dot(e.astype(BF), part(2)) * (1.0 / jnp.sum(e, axis=1, keepdims=True))
        lanes = pl.ds(pl.multiple_of(tile * 128, 128), 256)
        acc[rows, lanes] = jnp.where(own, o, acc[rows, lanes])

    def temporal_attend(start, count):
        def heads(j, _):
            for b in range(4):
                temporal_head(start, count, (4 * j + b) * HD)
            return 0

        lax.fori_loop(0, H // 4, heads, 0)
        rows = slice(start, start + count)
        return mid[rows] + mod[5:6] * dot(acc[rows].astype(BF), wto[...])

    acc[...] = jnp.zeros_like(acc)
    for i in (6, 7):
        loads[i].wait()
    arrived(tr, t_recv)
    mid[0:256] = tr[...].reshape(256, D).astype(F32)
    temporal_project(0, 256)
    to[...] = temporal_attend(0, 256).astype(BF).reshape(NF, 16, D)
    exchange(to, ro, u_send, u_recv)

    arrived(trh, th_recv)
    for j in range(NF):
        mid[256 + j * 8 : 264 + j * 8] = unpack(trh[j])
    temporal_project(256, 128)
    r = temporal_attend(256, 128)
    for j in range(NF):
        toh[j] = pack(r[j * 8 : j * 8 + 8])
    exchange(toh, roh, uh_send, uh_recv)

    arrived(ro, u_recv)
    for j in range(NF // 2):
        a, b = ro[2 * j].astype(F32), ro[2 * j + 1].astype(F32)
        for f in range(2):
            rows = jnp.concatenate([a[f * 8 : f * 8 + 8], b[f * 8 : f * 8 + 8]], 0)
            out[f, 16 * j : 16 * j + 16] = rows.astype(BF)
    arrived(roh, uh_recv)
    for j in range(NF // 4):
        a, b = (swap(unpack(roh[4 * j + i]), unpack(roh[4 * j + i + 1])) for i in (0, 2))
        for f in range(2):
            rows = jnp.concatenate([a[f], b[f]], 0)
            out[f, 128 + 16 * j : 144 + 16 * j] = rows.astype(BF)

    def sent_head(k, _):
        peer = at_head(k)
        for phase in range(4):
            for part in range(3):
                await_bytes(piece(phase, proj, part, peer), s_send.at[phase, part, peer])
        for kind in range(6):
            await_bytes(back_piece(kind, ot, peer), r_send.at[kind, peer])
        return 0

    lax.fori_loop(1, NH, sent_head, 0)

    def sent_frame(k, _):
        peer = at_frame(k)
        await_bytes(ts.at[peer], t_send.at[peer])
        await_bytes(tsh.at[peer], th_send.at[peer])
        await_bytes(to.at[peer], u_send.at[peer])
        await_bytes(toh.at[peer], uh_send.at[peer])
        return 0

    lax.fori_loop(1, NF, sent_frame, 0)


def local(latents, modulation, spatial_qkv, spatial_out, temporal_qkv, temporal_out):
    anywhere = pl.BlockSpec(memory_space=pl.ANY)
    vmem = pl.BlockSpec(memory_space=pltpu.VMEM)
    dma = pltpu.SemaphoreType.DMA
    return pl.pallas_call(
        kernel,
        out_shape=jax.ShapeDtypeStruct((2, PATCH, D), BF),
        in_specs=[anywhere, vmem] + [anywhere] * 5,
        out_specs=vmem,
        scratch_shapes=[
            pltpu.VMEM((2, PATCH, D), BF),
            pltpu.VMEM((3, TOK, D), F32),
            pltpu.VMEM((D, 3 * D), BF),
            pltpu.VMEM((D, D), BF),
            pltpu.VMEM((D, 3 * D), BF),
            pltpu.VMEM((D, D), BF),
            dma((8,)),
            pltpu.VMEM((TOK, D), BF),
            pltpu.VMEM((3, NH, PAIR, TOK), BF),
            pltpu.VMEM((3, NH, PAIR, TOK), BF),
            pltpu.VMEM((2, PAIR, KEYS), BF),
            pltpu.VMEM((2, PAIR + 32, KEYS), BF),
            pltpu.VMEM((6, 256, 80), BF),
            pltpu.VMEM((2, 256, KEYS), F32),
            pltpu.VMEM((2, 256, 96), BF),
            pltpu.VMEM((NH, PAIR, TOK), BF),
            pltpu.VMEM((NH, PAIR, TOK), BF),
            pltpu.VMEM((TOK, D), BF),
            pltpu.VMEM((NF, 16, D), BF),
            pltpu.VMEM((NF, 16, WIN), BF),
            pltpu.VMEM((NF, 16, D), BF),
            pltpu.VMEM((NF, 16, WIN), BF),
            pltpu.VMEM((TOK, D), F32),
            pltpu.VMEM((TOK, D), BF),
            pltpu.VMEM((TOK, 3 * D), BF),
            pltpu.VMEM((TOK, D), F32),
            pltpu.VMEM((NF, 16, D), BF),
            pltpu.VMEM((NF, 16, WIN), BF),
            pltpu.VMEM((NF, 16, D), BF),
            pltpu.VMEM((NF, 16, WIN), BF),
            pltpu.VMEM((2, 256, 256), F32),
            dma((4, 3, NH)), dma((4, 3, NH)), dma((6, NH)), dma((6, NH)),
            dma((NF,)), dma((NF,)), dma((NF,)), dma((NF,)),
            dma((NF,)), dma((NF,)), dma((NF,)), dma((NF,)),
        ],
        compiler_params=pltpu.CompilerParams(
            collective_id=0, has_side_effects=True, vmem_limit_bytes=62 * 2**20
        ),
    )(
        latents, modulation, jnp.asarray(rope_table()),
        spatial_qkv, spatial_out, temporal_qkv, temporal_out,
    )


def solution(mesh):
    return jax.shard_map(
        local,
        mesh=mesh,
        in_specs=(P("frame", "head", None), P(), P(), P(), P(), P()),
        out_specs=P("frame", "head", None),
        check_vma=False,
    )
```

time: 299 us -> 88.7 us (0.30)
  blocking collectives: 94.4 us -> 0 us
  Pallas kernels: 0 us -> 86.3 us
  local copies, waits for them, and re-layouts: 83.1 us -> 2.15 us
  matrix products: 58.6 us -> 0 us
  waiting for transfers between devices: 34.5 us -> 0 us
  other arithmetic: 15.6 us -> 0 us
  starting transfers between devices: 10.9 us -> 0 us
    all_to_all x3 -> x0, blocking collectives: 94.4 us -> none  [the longest x1 48.1 us: local(): lax.all_to_all(projected, 'head', split_axis=3, concat_axis=1, tiled=True)]
    pallas_call x0 -> x1, Pallas kernels: none -> 86.3 us  [local(): pl.pallas_call(kernel, out_shape=jax.ShapeDtypeStruct((2, PATCH, D), BF),...]
    reshape x6 -> x0, local copies, waits for them, and re-layouts: 41.6 us -> none  [the longest x2 20.9 us: local(): projected.astype(jnp.bfloat16)]
    dot_general x7 -> x0, matrix products: 38.2 us -> none  [the longest x2 14.6 us: attend(): jnp.einsum('bhqk,kbhe->qbhe', weights_bf, values, preferred_element_type=...]
    all_to_all x1 -> x0, waiting for transfers between devices: 34.5 us -> none  [local(): lax.all_to_all(projected_mid, 'frame', split_axis=1, concat_axis=0, tiled...]
    sub x1 -> x0, matrix products: 20.4 us -> none  [attend(): weights_bf = jax.nn.softmax(scores, axis=-1).astype(jnp.bfloat16)]
    another operation x3 -> x0, local copies, waits for them, and re-layouts: 19.2 us -> none  [the longest x1 13.2 us: temporal_heads(): pieces = projected.reshape(frames, patches, 3, heads_all, HD)]
    all_to_all x5 -> x0, local copies, waits for them, and re-layouts: 15.3 us -> none  [the longest x1 5.11 us: local(): lax.all_to_all(projected_mid, 'frame', split_axis=1, concat_axis=0, tiled...]
  transfers between devices with their start and end apart: 1 -> 0, of which waited for: 1 -> 0; matrix products, arithmetic and copies ran while one was open for 0% -> 0% of each run, Pallas kernels for 0% -> 0%
where the time goes in v2:
time: 88.7 us; the launch traced here: 88.5 us
  Pallas kernels  86.3 us (97%)
  local copies, waits for them, and re-layouts  2.15 us (2%)
    pallas_call x1, Pallas kernels, local(): pl.pallas_call(kernel, out_shape=jax.ShapeDtypeStruct((2, PATCH, D), BF),...  86.3 us
    unnamed x1, local copies, waits for them, and re-layouts  2.15 us

profile of v2, /device:TPU:1, one launch (start us, length us, event | category | flops | bytes accessed | tf_op | source)
XLA Modules:
  0.0 88.5 jit_solution(3602019856500247259)
XLA Ops:
  0.0 86.3 %shard_map.73 = bf16[2,192,1152]{2,1,0:T(8,128)(2,1)} custom-call(bf16[2,192,1152]{2,1,0:T(8,128)(2,1)} %lat_h.1, f32[6,1152]{1,0:T(8,128)} %mod.1, f32[3,384,1152]{2,1,0:T(8,128)} %constant.2.clone.tab_h, bf16[1152,3456]{1,0:T(8,128)(2,1)} %wsq_h.1, bf16[1152,1152]{1,0:T(8,128)(2,1)} %wso_h.1, bf16[1152,3456]{1,0:T(8,128)(2,1)} %wtq_h.1, ...), custom_call_target="tpu_custom_call" | custom-call | tf_op jit(solution)/shard_map/pallas_call | solution.py:420
  86.3 2.1 %copy.9 = bf16[2,192,1152]{2,1,0:T(8,128)(2,1)} copy(bf16[2,192,1152]{2,1,0:T(8,128)(2,1)} %shard_map.73) | data formatting | bytes 1769472

commit v3 on v2

--- a/solution.py
+++ b/solution.py
@@ -34,7 +34,10 @@
     cos = np.tile(np.concatenate([np.cos(angles)] * 2, 1), (1, H))
     low = np.tile(np.concatenate([-np.sin(angles), zeros], 1), (1, H))
     high = np.tile(np.concatenate([zeros, np.sin(angles)], 1), (1, H))
-    rows = [np.concatenate([np.repeat(t, 8, 0), np.repeat(t, 4, 0)], 0) for t in (cos, low, high)]
+    rows = [
+        np.concatenate([np.repeat(t[0::2], 8, 0), np.repeat(t[1::2], 8, 0), np.repeat(t, 4, 0)], 0)
+        for t in (cos, low, high)
+    ]
     return np.stack(rows).astype(np.float32)
 
 
@@ -48,8 +51,8 @@
     lat_h, mod, tab_h, wsq_h, wso_h, wtq_h, wto_h, out,
     lat, tab, wsq, wso, wtq, wto, load_sem,
     nrm, proj, recv, ks, vs, qs, sc, ob, ot, orecv, oa,
-    ts, tsh, tr, trh, mid, tin, tp, acc, to, toh, ro, roh, bias,
-    s_send, s_recv, r_send, r_recv, t_send, t_recv, th_send, th_recv,
+    ts, tr, mid, tin, tp, acc, to, toh, ro, roh, bias,
+    s_send, s_recv, r_send, r_recv, t_send, t_recv,
     u_send, u_recv, uh_send, uh_recv,
 ):
     fi, hi = lax.axis_index("frame"), lax.axis_index("head")
@@ -247,12 +250,6 @@
 
         lax.fori_loop(0, 3, body, 0)
 
-    for f in range(2):
-        for h in range(2):
-            attend(f, h)
-
-    for i in (1, 5):
-        loads[i].wait()
     sub = lax.broadcasted_iota(jnp.int32, (8, D), 0)
 
     def swap(a, b):
@@ -268,32 +265,26 @@
         return jnp.concatenate([x[0:8], x[8:16, 2 * WIN - D : WIN]], 1)
 
     def finish_spatial(kind):
-        kinds = ((0, 1, 4, 5), (2, 3))[kind]
+        tile = (0, 2, 1)[kind]
 
         def arrive(src, _):
-            for one in kinds:
-                await_bytes(back_piece(one, orecv, src), r_recv.at[one, src])
+            for h in range(2):
+                await_bytes(back_piece(2 * tile + h, orecv, src), r_recv.at[2 * tile + h, src])
             return 0
 
         lax.fori_loop(0, NH, arrive, 0)
-        start, count = ((0, 256), (256, 128))[kind]
-        for t, at in enumerate(((0, 256), (128,))[kind]):
-            row = start + t * 128
-            oa[row : row + 128] = orecv[:, :, at : at + 128].reshape(D, 128).T
-        r = dot(oa[start : start + count], wso[...])
-        half = count // 2
-        first = 128 * kind
-        fresh = []
-        for f in range(2):
-            x = lat[f, first : first + half].astype(F32)
-            fresh.append(x + mod[2:3] * r[f * half : (f + 1) * half])
-        for g in range(half // 8):
-            a, b = (x[g * 8 : g * 8 + 8] for x in fresh)
-            if kind == 0:
-                ts[g] = jnp.concatenate([a, b], 0).astype(BF)
-            else:
-                a, b = swap(a, b)
-                tsh[2 * g], tsh[2 * g + 1] = pack(a), pack(b)
+        rows = slice(kind * 128, kind * 128 + 128)
+        oa[rows] = orecv[:, :, tile * 128 : tile * 128 + 128].reshape(D, 128).T
+        r = mod[2:3] * dot(oa[rows], wso[...])
+        if kind < 2:
+            r = lat[kind, 0:128].astype(F32) + r
+            for g in range(NF):
+                ts[kind, g] = pack(r[g * 8 : g * 8 + 8])
+        else:
+            x = [lat[f, 128:PATCH].astype(F32) + r[f * 64 : f * 64 + 64] for f in range(2)]
+            for g in range(NF // 2):
+                a, b = swap(*(y[g * 8 : g * 8 + 8] for y in x))
+                ts[2, 2 * g], ts[2, 2 * g + 1] = pack(a), pack(b)
 
     def exchange(source, target, send, receive):
         pltpu.make_async_copy(source.at[fi], target.at[fi], receive.at[fi]).start()
@@ -314,11 +305,6 @@
             return 0
 
         lax.fori_loop(0, NF, one, 0)
-
-    finish_spatial(0)
-    exchange(ts, tr, t_send, t_recv)
-    finish_spatial(1)
-    exchange(tsh, trh, th_send, th_recv)
 
     def temporal_project(start, count):
         rows = slice(start, start + count)
@@ -347,32 +333,51 @@
         s = s + bias[0 if count == 256 else 1, 0:count, 0:count]
         e = jnp.exp2((s - jnp.max(s, axis=1, keepdims=True)) * SCALE)
         o = dot(e.astype(BF), part(2)) * (1.0 / jnp.sum(e, axis=1, keepdims=True))
-        lanes = pl.ds(pl.multiple_of(tile * 128, 128), 256)
-        acc[rows, lanes] = jnp.where(own, o, acc[rows, lanes])
+        return own, o, pl.ds(pl.multiple_of(tile * 128, 128), 256)
 
     def temporal_attend(start, count):
+        group = 4 if count == 256 else 8
+        rows = slice(start, start + count)
+
         def heads(j, _):
-            for b in range(4):
-                temporal_head(start, count, (4 * j + b) * HD)
-            return 0
-
-        lax.fori_loop(0, H // 4, heads, 0)
-        rows = slice(start, start + count)
+            done = [temporal_head(start, count, (group * j + b) * HD) for b in range(group)]
+            for own, o, lanes in done:
+                acc[rows, lanes] = jnp.where(own, o, acc[rows, lanes])
+            return 0
+
+        lax.fori_loop(0, H // group, heads, 0)
         return mid[rows] + mod[5:6] * dot(acc[rows].astype(BF), wto[...])
 
+    def give_piece(kind):
+        finish_spatial(kind)
+        exchange(ts.at[kind], tr.at[kind], t_send.at[kind], t_recv.at[kind])
+
+    def take_piece(kind):
+        arrived(tr.at[kind], t_recv.at[kind])
+        for j in range(NF):
+            mid[kind * 128 + j * 8 : kind * 128 + j * 8 + 8] = unpack(tr[kind, j])
+        temporal_project(kind * 128, 128)
+
+    attend(0, 0)
+    attend(0, 1)
+    attend(1, 0)
+    for i in (1, 5):
+        loads[i].wait()
+    give_piece(0)
+    attend(1, 1)
+    give_piece(1)
+    give_piece(2)
     acc[...] = jnp.zeros_like(acc)
     for i in (6, 7):
         loads[i].wait()
-    arrived(tr, t_recv)
-    mid[0:256] = tr[...].reshape(256, D).astype(F32)
-    temporal_project(0, 256)
-    to[...] = temporal_attend(0, 256).astype(BF).reshape(NF, 16, D)
+    take_piece(0)
+    take_piece(1)
+    r = temporal_attend(0, 256)
+    for j in range(NF):
+        both = [r[f * 128 + j * 8 : f * 128 + j * 8 + 8] for f in range(2)]
+        to[j] = jnp.concatenate(both, 0).astype(BF)
     exchange(to, ro, u_send, u_recv)
-
-    arrived(trh, th_recv)
-    for j in range(NF):
-        mid[256 + j * 8 : 264 + j * 8] = unpack(trh[j])
-    temporal_project(256, 128)
+    take_piece(2)
     r = temporal_attend(256, 128)
     for j in range(NF):
         toh[j] = pack(r[j * 8 : j * 8 + 8])
@@ -404,8 +409,8 @@
 
     def sent_frame(k, _):
         peer = at_frame(k)
-        await_bytes(ts.at[peer], t_send.at[peer])
-        await_bytes(tsh.at[peer], th_send.at[peer])
+        for kind in range(3):
+            await_bytes(ts.at[kind, peer], t_send.at[kind, peer])
         await_bytes(to.at[peer], u_send.at[peer])
         await_bytes(toh.at[peer], uh_send.at[peer])
         return 0
@@ -441,10 +446,8 @@
             pltpu.VMEM((NH, PAIR, TOK), BF),
             pltpu.VMEM((NH, PAIR, TOK), BF),
             pltpu.VMEM((TOK, D), BF),
-            pltpu.VMEM((NF, 16, D), BF),
-            pltpu.VMEM((NF, 16, WIN), BF),
-            pltpu.VMEM((NF, 16, D), BF),
-            pltpu.VMEM((NF, 16, WIN), BF),
+            pltpu.VMEM((3, NF, 16, WIN), BF),
+            pltpu.VMEM((3, NF, 16, WIN), BF),
             pltpu.VMEM((TOK, D), F32),
             pltpu.VMEM((TOK, D), BF),
             pltpu.VMEM((TOK, 3 * D), BF),
@@ -455,8 +458,8 @@
             pltpu.VMEM((NF, 16, WIN), BF),
             pltpu.VMEM((2, 256, 256), F32),
             dma((4, 3, NH)), dma((4, 3, NH)), dma((6, NH)), dma((6, NH)),
-            dma((NF,)), dma((NF,)), dma((NF,)), dma((NF,)),
-            dma((NF,)), dma((NF,)), dma((NF,)), dma((NF,)),
+            dma((3, NF)), dma((3, NF)), dma((NF,)), dma((NF,)),
+            dma((NF,)), dma((NF,)),
         ],
         compiler_params=pltpu.CompilerParams(
             collective_id=0, has_side_effects=True, vmem_limit_bytes=62 * 2**20

time: 88.7 us -> 88 us (level)
  no operation moved by 1% of the time
where the time goes in v3:
time: 88 us; the launch traced here: 87.8 us
  Pallas kernels  85.6 us (97%)
  local copies, waits for them, and re-layouts  2.15 us (2%)
    pallas_call x1, Pallas kernels, local(): pl.pallas_call(kernel, out_shape=jax.ShapeDtypeStruct((2, PATCH, D), BF),...  85.6 us
    unnamed x1, local copies, waits for them, and re-layouts  2.15 us

profile of v3, /device:TPU:1, one launch (start us, length us, event | category | flops | bytes accessed | tf_op | source)
XLA Modules:
  0.0 87.8 jit_solution(10545612918741676961)
XLA Ops:
  0.0 85.6 %shard_map.73 = bf16[2,192,1152]{2,1,0:T(8,128)(2,1)} custom-call(bf16[2,192,1152]{2,1,0:T(8,128)(2,1)} %lat_h.1, f32[6,1152]{1,0:T(8,128)} %mod.1, f32[3,384,1152]{2,1,0:T(8,128)} %constant.2.clone.tab_h, bf16[1152,3456]{1,0:T(8,128)(2,1)} %wsq_h.1, bf16[1152,1152]{1,0:T(8,128)(2,1)} %wso_h.1, bf16[1152,3456]{1,0:T(8,128)(2,1)} %wtq_h.1, ...), custom_call_target="tpu_custom_call" | custom-call | tf_op jit(solution)/shard_map/pallas_call | solution.py:425
  85.6 2.1 %copy.9 = bf16[2,192,1152]{2,1,0:T(8,128)(2,1)} copy(bf16[2,192,1152]{2,1,0:T(8,128)(2,1)} %shard_map.73) | data formatting | bytes 1769472

commit v4 on v3

--- a/solution.py
+++ b/solution.py
@@ -320,32 +320,29 @@
 
     def temporal_head(start, count, offset):
         rows = slice(start, start + count)
-        tile = jnp.minimum(offset // 128, 7)
+        tile = min(offset // 128, 7)
         begin = offset - tile * 128
         lane = lax.broadcasted_iota(jnp.int32, (count, 256), 1)
         own = (lane >= begin) & (lane < begin + HD)
 
         def part(i):
-            return tp[rows, pl.ds(pl.multiple_of(i * D + tile * 128, 128), 256)]
+            return tp[rows, pl.ds(i * D + tile * 128, 256)]
 
         q = part(0)
         s = dot(jnp.where(own, q, jnp.zeros_like(q)), part(1), NT)
         s = s + bias[0 if count == 256 else 1, 0:count, 0:count]
         e = jnp.exp2((s - jnp.max(s, axis=1, keepdims=True)) * SCALE)
         o = dot(e.astype(BF), part(2)) * (1.0 / jnp.sum(e, axis=1, keepdims=True))
-        return own, o, pl.ds(pl.multiple_of(tile * 128, 128), 256)
+        return own, o, pl.ds(tile * 128, 256)
 
     def temporal_attend(start, count):
-        group = 4 if count == 256 else 8
+        group = 4
         rows = slice(start, start + count)
 
-        def heads(j, _):
+        for j in range(H // group):
             done = [temporal_head(start, count, (group * j + b) * HD) for b in range(group)]
             for own, o, lanes in done:
                 acc[rows, lanes] = jnp.where(own, o, acc[rows, lanes])
-            return 0
-
-        lax.fori_loop(0, H // group, heads, 0)
         return mid[rows] + mod[5:6] * dot(acc[rows].astype(BF), wto[...])
 
     def give_piece(kind):

time: 88 us -> 86 us (0.977)
  Pallas kernels: 85.6 us -> 83.7 us
    pallas_call x1, Pallas kernels: 85.6 us -> 83.7 us  [local(): pl.pallas_call(kernel, out_shape=jax.ShapeDtypeStruct((2, PATCH, D), BF),...]
where the time goes in v4:
time: 86 us; the launch traced here: 85.8 us
  Pallas kernels  83.7 us (97%)
  local copies, waits for them, and re-layouts  2.15 us (2%)
    pallas_call x1, Pallas kernels, local(): pl.pallas_call(kernel, out_shape=jax.ShapeDtypeStruct((2, PATCH, D), BF),...  83.7 us
    unnamed x1, local copies, waits for them, and re-layouts  2.15 us

profile of v4, /device:TPU:1, one launch (start us, length us, event | category | flops | bytes accessed | tf_op | source)
XLA Modules:
  0.0 85.8 jit_solution(4478021093775914587)
XLA Ops:
  0.0 83.7 %shard_map.73 = bf16[2,192,1152]{2,1,0:T(8,128)(2,1)} custom-call(bf16[2,192,1152]{2,1,0:T(8,128)(2,1)} %lat_h.1, f32[6,1152]{1,0:T(8,128)} %mod.1, f32[3,384,1152]{2,1,0:T(8,128)} %constant.2.clone.tab_h, bf16[1152,3456]{1,0:T(8,128)(2,1)} %wsq_h.1, bf16[1152,1152]{1,0:T(8,128)(2,1)} %wso_h.1, bf16[1152,3456]{1,0:T(8,128)(2,1)} %wtq_h.1, ...), custom_call_target="tpu_custom_call" | custom-call | tf_op jit(solution)/shard_map/pallas_call | solution.py:422
  83.7 2.1 %copy.9 = bf16[2,192,1152]{2,1,0:T(8,128)(2,1)} copy(bf16[2,192,1152]{2,1,0:T(8,128)(2,1)} %shard_map.73) | data formatting | bytes 1769472
